TPU v7x, 32 devices: a whole 2x2x4 slice. The times are simulated.
32 devices in a mesh: groups: 2 (over x), chan: 16 (over z, y, core), freq: 1.
Axes of the slice: x: 2, y: 2, z: 4, core: 2. Of those that a mesh axis runs over, the one named last changes fastest.
Arguments:
- raw: bfloat16 [256, 16, 12000], P(('groups', 'chan'), 'freq'), parts along dimension 0, may hold values from -100 to 100, as said below
- lengths: int32 [256, 16], P(('groups', 'chan'), 'freq'), parts along dimension 0, may hold values from 6000 to 12000
- quality: int32 [256], P('groups'), parts along dimension 0, may hold values 0 or 1
- assignment: int32 [256], P('groups'), parts along dimension 0, may hold values from 0 to 127, as said below
Outputs:
- cross: bfloat16 [512, 256, 2, 128], P('freq', ('groups', 'chan')), parts along dimension 1
There are 2 independent parts, one for each index of `groups`. A program takes and returns all parts, laid end to end along the dimension named above; each array names one. Nothing has to cross between parts.
Inputs may be any that keep to these rules, and one draw needn't show every extreme that they name: `raw`: records are clipped to this range. `assignment`: A permutation. The 8 channels of one file block (consecutive entries) land at most 1 in any one block of 8 consecutive positions, and some pair of blocks reaches 1.
All inputs are finite; a program needn't handle non-finite values.
Results may differ from a plain program's by a relative error of at most 0.012.
The roundings to bfloat16 on the way count: a program that leaves them out, or rounds other values in their place, can miss the bound.
Values may be sent and summed in bfloat16 or wider, within the bound.
A program may use at most 128 MiB of HBM per device.

v0:
```python
import math

import jax
import jax.numpy as jnp
from jax import lax
from jax.sharding import PartitionSpec as P

WIN = 12000
NB = 512
K0 = 6
SUB = 32


def dft_table(first_sample, sample_count):
    samples = first_sample + jnp.arange(sample_count, dtype=jnp.int32)
    bin_index = K0 + jnp.arange(NB, dtype=jnp.int32)
    residue = samples[:, None] * bin_index[None, :] % WIN
    angles = residue.astype(jnp.float32) * (2.0 * math.pi / WIN)
    return jnp.concatenate([jnp.cos(angles), -jnp.sin(angles)], axis=1).astype(jnp.bfloat16)


def prepare(raw_block, valid_lengths):
    positions = jnp.arange(WIN, dtype=jnp.int32)
    inside = positions[None, None, :] < valid_lengths[:, :, None]
    values = raw_block.astype(jnp.float32)
    kept = jnp.where(inside, values, 0.0)
    average = jnp.sum(kept, axis=-1) / valid_lengths.astype(jnp.float32)
    taper = 0.5 - 0.5 * jnp.cos(positions.astype(jnp.float32) * (2.0 * math.pi / WIN))
    return jnp.where(inside, (values - average[:, :, None]) * taper[None, None, :], 0.0).astype(
        jnp.bfloat16
    )


def whiten(spectra):
    row_count = spectra.shape[0]
    grouped = spectra.reshape(row_count, 2, NB // SUB, SUB)
    power = jnp.sum(grouped * grouped, axis=(1, 3)) / SUB
    factor = lax.rsqrt(power + 1e-06)
    return (grouped * factor[:, None, :, None]).reshape(row_count, 2, NB).astype(jnp.bfloat16)


def spectra_of(shaped_rows):
    row_count = shaped_rows.shape[0]
    pieces = 8
    block_width = WIN // pieces
    total = jnp.zeros((row_count, 2 * NB), jnp.float32)
    for block_index in range(pieces):
        first_sample = block_index * block_width
        segment = lax.slice_in_dim(shaped_rows, first_sample, first_sample + block_width, axis=1)
        total = total + jnp.dot(
            segment, dft_table(first_sample, block_width), preferred_element_type=jnp.float32
        )
    return whiten(total)


def cross_block(left_rows, right_rows, all_windows):
    bins_here = left_rows.shape[3]
    left_side = left_rows.transpose(3, 0, 2, 1).reshape(
        bins_here, left_rows.shape[0], 2 * all_windows
    )
    right_count = right_rows.shape[0]
    right_plain = right_rows.transpose(3, 2, 1, 0).reshape(bins_here, 2 * all_windows, right_count)
    turned = jnp.stack([-right_rows[:, :, 1], right_rows[:, :, 0]], axis=2)
    right_turned = turned.transpose(3, 2, 1, 0).reshape(bins_here, 2 * all_windows, right_count)
    real_part = jnp.einsum(
        "bik,bkj->bij", left_side, right_plain, preferred_element_type=jnp.float32
    )
    imag_part = jnp.einsum(
        "bik,bkj->bij", left_side, right_turned, preferred_element_type=jnp.float32
    )
    return (jnp.stack([real_part, imag_part], axis=2) / all_windows).astype(jnp.bfloat16)


def body(raw, lengths, quality, assignment):
    channel_count = lax.axis_size("chan")
    my_index = lax.axis_index("chan")
    block_rows, window_count, sample_count = raw.shape
    capacity = max(1, block_rows // channel_count)
    total_channels = assignment.shape[0]
    targets_all = assignment.reshape(channel_count, block_rows) // block_rows
    row_numbers = jnp.arange(block_rows, dtype=jnp.int32)
    same_target = targets_all[:, :, None] == targets_all[:, None, :]
    earlier = row_numbers[None, None, :] < row_numbers[None, :, None]
    slot_table = jnp.sum(jnp.logical_and(same_target, earlier), axis=2)
    quality_table = quality.reshape(channel_count, block_rows)
    my_targets = lax.dynamic_index_in_dim(targets_all, my_index, 0, keepdims=False)
    my_slots = lax.dynamic_index_in_dim(slot_table, my_index, 0, keepdims=False)
    my_quality = lax.dynamic_index_in_dim(quality_table, my_index, 0, keepdims=False)
    device_numbers = jnp.arange(channel_count, dtype=jnp.int32)
    slot_numbers = jnp.arange(capacity, dtype=jnp.int32)
    match_table = jnp.logical_and(
        jnp.logical_and(
            my_targets[None, None, :] == device_numbers[:, None, None],
            my_slots[None, None, :] == slot_numbers[None, :, None],
        ),
        my_quality[None, None, :] == 1,
    )
    present = jnp.any(match_table, axis=2).reshape(-1)
    source_row = jnp.sum(jnp.where(match_table, row_numbers[None, None, :], 0), axis=2).reshape(-1)
    inverse = (
        jnp.zeros((total_channels,), jnp.int32)
        .at[assignment]
        .set(jnp.arange(total_channels, dtype=jnp.int32))
    )
    arrivals = lax.dynamic_slice_in_dim(inverse, my_index * block_rows, block_rows)
    source_device = arrivals // block_rows
    flat_slot = source_device * capacity + jnp.take(slot_table.reshape(-1), arrivals)
    arrival_good = jnp.take(quality, arrivals)
    shaped = prepare(raw, lengths)
    picked = jnp.take(shaped, source_row, axis=0)
    kept_rows = picked * present.astype(shaped.dtype).reshape((-1,) + (1,) * (shaped.ndim - 1))
    arrived = lax.all_to_all(
        kept_rows.reshape((channel_count, capacity) + shaped.shape[1:]),
        "chan",
        split_axis=0,
        concat_axis=0,
        tiled=True,
    )
    flat_rows = arrived.reshape((channel_count * capacity,) + arrived.shape[2:])
    picked = jnp.take(flat_rows, flat_slot, axis=0)
    local_rows = picked * arrival_good.astype(arrived.dtype).reshape(
        (-1,) + (1,) * (arrived.ndim - 2)
    )
    whitened = spectra_of(local_rows.reshape(block_rows * window_count, sample_count)).reshape(
        block_rows, window_count, 2, NB
    )
    panel = lax.all_to_all(whitened, "freq", split_axis=3, concat_axis=1, tiled=True)
    all_windows = panel.shape[1]
    return cross_block(panel, lax.all_gather(panel, "chan", axis=0, tiled=True), all_windows)


def solution(mesh):
    return jax.shard_map(
        body,
        mesh=mesh,
        in_specs=(
            P(("groups", "chan"), "freq", None),
            P(("groups", "chan"), "freq"),
            P("groups"),
            P("groups"),
        ),
        out_specs=P("freq", ("groups", "chan"), None, None),
        check_vma=False,
    )
```

profile of v0, /device:TPU:0, one launch (start us, length us, event | category | flops | bytes accessed | tf_op | source)
XLA Modules:
  0.0 277.3 jit_solution(14290823064365634316)
XLA Ops:
  8.8 3.3 %fusion = f32[8,16]{1,0:T(8,128)S(1)} fusion(bf16[8,16,12000]{2,1,0:T(8,128)(2,1)} %param.6, s32[8,16]{1,0:T(8,128)} %param.7), kind=kLoop, calls=%fused_computation.7 | loop fusion | flops 6143872 | bytes 3073024 | tf_op jit(solution)/shard_map/reduce_sum | solution.py:27
  12.1 1.5 fusion.3
  13.6 3.5 %gather_fusion = bf16[16,16,12000]{2,1,0:T(8,128)(2,1)} fusion(bf16[8,16,12000]{2,1,0:T(8,128)(2,1)S(1)} %fusion.3, s32[1024]{0:T(1024)S(1)} %pad_clamp_fusion.1), kind=kCustom, calls=%fused_computation.2 | custom fusion | bytes 12288064 | tf_op jit(solution)/shard_map/jit(_take)/gather | solution.py:110
  17.2 6.0 %fusion.4 = bf16[16,1,16,12000]{3,2,1,0:T(8,128)(2,1)} fusion(bf16[16,16,12000]{2,1,0:T(8,128)(2,1)} %gather_fusion, pred[16]{0:T(512)(128)(4,1)S(1)} %compare_and_fusion.1, bf16[16]{0:T(256)(128)(2,1)S(1)} %convert_element_type.89), kind=kLoop, calls=%fused_computation.12 | loop fusion | flops 6144000 | bytes 12288048 | tf_op jit(solution)/shard_map/mul | solution.py:111
  23.1 7.6 %all-to-all-start = ((bf16[16,1,16,12000]{3,2,1,0:T(8,128)(2,1)}), bf16[16,1,16,12000]{3,2,1,0:T(8,128)(2,1)}, u32[]{:S(2)}, u32[]{:S(2)}) async-start(bf16[16,1,16,12000]{3,2,1,0:T(8,128)(2,1)} %fusion.4), calls=%async_computation | async-start | bytes 12320768 | tf_op jit(solution)/shard_map/all_to_all | solution.py:112
  30.8 1.2 scatter_custom_fusion
  34.0 109.5 %cosine_convert_fusion = (bf16[1500,512]{1,0:T(8,128)(2,1)}, bf16[1500,512]{1,0:T(8,128)(2,1)}, bf16[1500,512]{1,0:T(8,128)(2,1)}, bf16[1500,512]{1,0:T(8,128)(2...) fusion(s32[1500]{0:T(1024)S(1)} %get-tuple-element.40, ...), kind=kLoop, calls=%fused_computation.76 | loop fusion | flops 73728000 | bytes 24620048 | tf_op jit(solution)/shard_map/convert
  143.6 3.5 %gather_fusion.1 = bf16[8,16,12000]{2,1,0:T(8,128)(2,1)S(1)} fusion(bf16[16,16,12000]{2,1,0:T(8,128)(2,1)} %bitcast.5, s32[1024]{0:T(1024)S(1)} %pad_clamp_fusion), kind=kCustom, calls=%fused_computation.3 | custom fusion | bytes 6144032 | tf_op jit(solution)/shard_map/jit(_take)/gather | solution.py:120
  147.6 0.9 copy-done.17
  149.5 0.8 copy-done.15
  151.4 0.8 copy-done.13
  153.3 0.8 copy-done.11
  158.9 0.8 copy-done.5
  160.7 0.8 copy-done.3
  164.2 0.8 fusion.100
  165.0 1.7 copy.42
  166.7 70.9 %all-gather.2.cloned.1.call-done = bf16[128,16,2,512]{3,1,2,0:T(8,128)(2,1)} async-done(((bf16[8,16,2,512]{3,1,2,0:T(8,128)(2,1)}), bf16[128,16,2,512]{3,1,2,0:T(8,128)(2,1)}) %all-gather.2.cloned.1.call-update) | async-done | bytes 4194320 | tf_op jit(solution)/shard_map/all_gather | solution.py:129
  237.6 9.1 %copy.41 = bf16[512,2,16,128]{3,2,1,0:T(8,128)(2,1)} copy(bf16[512,2,16,128]{0,2,1,3:T(8,128)(2,1)} %bitcast.37) | data formatting | bytes 8388608 | tf_op jit(solution)/shard_map/transpose | solution.py:62
  246.7 2.5 slice_negate_fusion
  249.2 2.3 maximum_bitcast_fusion
  251.6 9.1 %copy.43 = bf16[512,2,16,128]{3,2,1,0:T(8,128)(2,1)} copy(bf16[512,2,16,128]{0,2,1,3:T(8,128)(2,1)} %maximum_bitcast_fusion) | data formatting | bytes 8388608 | tf_op jit(solution)/shard_map/transpose | solution.py:64
  260.7 3.5 %convolution_bitcast_fusion.1 = f32[512,8,1,128]{3,1,0,2:T(8,128)S(1)} fusion(bf16[512,8,32]{2,1,0:T(8,128)(2,1)S(1)} %copy.42, bf16[512,32,128]{2,1,0:T(8,128)(2,1)} %bitcast.35), kind=kOutput, calls=%fused_computation.125 | convolution fusion | flops 33554432 | bytes 6553600 | tf_op jit(solution)/shard_map/bik,bkj->bij/dot_general | solution.py:65
  264.3 1.3 convolution_bitcast_fusion
  265.9 4.6 %copy.45 = bf16[512,8,2,128]{3,2,1,0:T(2,128)(2,1)} copy(bf16[512,8,2,128]{3,1,0,2:T(8,128)(2,1)S(1)} %fusion.5) | data formatting | bytes 4194304 | tf_op jit(solution)/shard_map/convert_element_type | solution.py:71
  (93 shorter events, 17.0 us)
Async XLA Ops:
  6.5 5.5 %copy-start.19 = (s32[8,16]{1,0:T(8,128)S(1)}, s32[8,16]{1,0:T(8,128)}, u32[]{:S(2)}) copy-start(s32[8,16]{1,0:T(8,128)} %param.7) | copy-start | bytes 1540
  8.1 4.0 %copy-start.2 = (bf16[8,16,12000]{2,1,0:T(8,128)(2,1)S(1)}, bf16[8,16,12000]{2,1,0:T(8,128)(2,1)}, u32[]{:S(2)}) copy-start(bf16[8,16,12000]{2,1,0:T(8,128)(2,1)} %param.6) | copy-start | bytes 9216004
  23.1 7.7 %copy-start.20 = (s32[128]{0:T(128)S(1)}, s32[128]{0:T(128)}, u32[]{:S(2)}) copy-start(s32[128]{0:T(128)} %param.9) | copy-start | bytes 1540
  23.1 9.0 %copy-start = (s32[128]{0:T(128)S(1)}, s32[128]{0:T(128)}, u32[]{:S(2)}) copy-start(s32[128]{0:T(128)} %param.8) | copy-start | bytes 1540
  23.1 120.4 %all-to-all-start = ((bf16[16,1,16,12000]{3,2,1,0:T(8,128)(2,1)}), bf16[16,1,16,12000]{3,2,1,0:T(8,128)(2,1)}, u32[]{:S(2)}, u32[]{:S(2)}) async-start(bf16[16,1,16,12000]{3,2,1,0:T(8,128)(2,1)} %fusion.4), calls=%async_computation | async-start | bytes 12320768 | tf_op jit(solution)/shard_map/all_to_all | solution.py:112
  30.7 206.9 %all-gather.2.cloned.1.call-start = ((), (), s32[]{:S(2)}) async-start(), calls=%async_computation.1 | async-start | bytes 4456448 | tf_op jit(solution)/shard_map/all_gather | solution.py:129
  147.1 1.4 copy-start.17
  147.1 1.9 copy-start.18
  148.9 1.4 copy-start.15
  148.9 1.9 copy-start.16
  150.8 1.4 copy-start.13
  150.8 1.9 copy-start.14
  152.7 1.4 copy-start.11
  152.7 1.9 copy-start.12
  154.5 1.4 copy-start.9
  154.5 1.9 copy-start.10
  156.4 1.4 copy-start.7
  156.4 1.9 copy-start.8
  158.2 1.4 copy-start.5
  158.2 1.9 copy-start.6
  160.1 1.4 copy-start.3
  160.1 1.9 copy-start.4
  260.7 3.5 %copy-start.1 = (bf16[512,2,16,128]{3,2,1,0:T(8,128)(2,1)S(1)}, bf16[512,2,16,128]{3,2,1,0:T(8,128)(2,1)}, u32[]{:S(2)}) copy-start(bf16[512,2,16,128]{3,2,1,0:T(8,128)(2,1)} %copy.43) | copy-start | bytes 12582916
Sparse Core Ops, SparseCore 0:
  165.1 72.4 all-gather.1
where the time goes:
time: 278 us; the launch traced here: 277 us
  other arithmetic  128 us (46%)
  waiting for transfers between devices  70.9 us (26%)
  local copies, waits for them, and re-layouts  47.6 us (17%)
  between operations  13.7 us (5%)
  matrix products  9.74 us (4%)
  starting transfers between devices  7.6 us (3%)
    another operation x1, other arithmetic  110 us
    all_gather x1, waiting for transfers between devices, body(): lax.all_gather(panel, 'chan', axis=0, tiled=True)  70.9 us
    unnamed x42, local copies, waits for them, and re-layouts  9.99 us
    transpose x1, local copies, waits for them, and re-layouts, cross_block(): turned.transpose(3, 2, 1, 0)  9.15 us
    transpose x1, local copies, waits for them, and re-layouts, cross_block(): right_rows.transpose(3, 2, 1, 0)  9.12 us
    all_to_all x1, starting transfers between devices, body(): lax.all_to_all(kept_rows.reshape((channel_count, capacity) + shaped.shape...  7.56 us
    mul x1, other arithmetic, body(): picked * present.astype(shaped.dtype).reshape((-1,) + (1,) * (shaped.ndim...  5.97 us
  transfers between devices with their start and end apart: 2, of which 1 were waited for; matrix products, arithmetic and copies ran while one was open for 41% of the time, Pallas kernels for 0%

commit v1 on v0

v1 whole, which is shorter than its diff:
```python
import math

import jax
import jax.numpy as jnp
import ml_dtypes
import numpy as np
from jax import lax
from jax.sharding import PartitionSpec as P

WIN = 12000
NB = 512
K0 = 6
SUB = 32
QUARTER = WIN // 4


def quarter_table():
    samples = np.arange(QUARTER, dtype=np.int64)
    bins = K0 + np.arange(NB, dtype=np.int64)
    residue = samples[:, None] * bins[None, :] % WIN
    angles = residue.astype(np.float32) * np.float32(2.0 * math.pi / WIN)
    real = np.cos(angles).astype(ml_dtypes.bfloat16)
    imag = (-np.sin(angles)).astype(ml_dtypes.bfloat16)
    return real, imag


def turns():
    power = (np.arange(4)[:, None] * (K0 + np.arange(NB))[None, :]) % 4
    real = np.array([1.0, 0.0, -1.0, 0.0], np.float32)[power]
    imag = np.array([0.0, -1.0, 0.0, 1.0], np.float32)[power]
    return real, imag


def prepare(raw_block, valid_lengths):
    positions = jnp.arange(WIN, dtype=jnp.int32)
    inside = positions[None, None, :] < valid_lengths[:, :, None]
    values = raw_block.astype(jnp.float32)
    kept = jnp.where(inside, values, 0.0)
    average = jnp.sum(kept, axis=-1) / valid_lengths.astype(jnp.float32)
    taper = 0.5 - 0.5 * jnp.cos(positions.astype(jnp.float32) * (2.0 * math.pi / WIN))
    return jnp.where(inside, (values - average[:, :, None]) * taper[None, None, :], 0.0).astype(
        jnp.bfloat16
    )


def whiten(spectra):
    row_count = spectra.shape[0]
    grouped = spectra.reshape(row_count, 2, NB // SUB, SUB)
    power = jnp.sum(grouped * grouped, axis=(1, 3)) / SUB
    factor = lax.rsqrt(power + 1e-06)
    return (grouped * factor[:, None, :, None]).reshape(row_count, 2, NB).astype(jnp.bfloat16)


def spectra_of(shaped_rows):
    row_count = shaped_rows.shape[0]
    real_table, imag_table = quarter_table()
    table = jnp.asarray(np.concatenate([real_table, imag_table], axis=1))
    quarters = jnp.concatenate(
        [lax.slice_in_dim(shaped_rows, q * QUARTER, (q + 1) * QUARTER, axis=1) for q in range(4)], axis=0
    )
    parts = jnp.dot(quarters, table, preferred_element_type=jnp.float32).reshape(4, row_count, 2, NB)
    turn_real, turn_imag = (jnp.asarray(t)[:, None, :] for t in turns())
    real = jnp.sum(parts[:, :, 0] * turn_real - parts[:, :, 1] * turn_imag, axis=0)
    imag = jnp.sum(parts[:, :, 1] * turn_real + parts[:, :, 0] * turn_imag, axis=0)
    return whiten(jnp.concatenate([real, imag], axis=1))


def plain_body(raw, lengths, quality, assignment):
    my_index = lax.axis_index("chan")
    block_rows, window_count, sample_count = raw.shape
    total_channels = assignment.shape[0]
    my_quality = lax.dynamic_slice_in_dim(quality, my_index * block_rows, block_rows)
    shaped = prepare(raw, lengths)
    whitened = spectra_of(shaped.reshape(block_rows * window_count, sample_count)).reshape(
        block_rows, window_count, 2, NB
    )
    whitened = whitened * my_quality.astype(jnp.bfloat16)[:, None, None, None]
    panel = lax.all_to_all(whitened, "freq", split_axis=3, concat_axis=1, tiled=True)
    all_windows = panel.shape[1]
    gathered = lax.all_gather(panel, "chan", axis=0, tiled=True)
    positions = jnp.arange(total_channels, dtype=jnp.int32)
    place = (assignment[:, None] == positions[None, :]).astype(jnp.bfloat16)
    my_positions = my_index * block_rows + jnp.arange(block_rows, dtype=jnp.int32)
    my_place = (assignment[:, None] == my_positions[None, :]).astype(jnp.bfloat16)
    bins_here = gathered.shape[3]
    right = jnp.einsum("cwpb,cj->bpwj", gathered, place, preferred_element_type=jnp.float32)
    right = right.astype(jnp.bfloat16).reshape(bins_here, 2 * all_windows, total_channels)
    left = jnp.einsum("cwpb,ci->bipw", gathered, my_place, preferred_element_type=jnp.float32)
    left = left.astype(jnp.bfloat16)
    both = jnp.stack(
        [left, jnp.stack([left[:, :, 1], -left[:, :, 0]], axis=2)], axis=2
    ).reshape(bins_here, 2 * block_rows, 2 * all_windows)
    cross = jnp.einsum("bik,bkj->bij", both, right, preferred_element_type=jnp.float32)
    return (cross / all_windows).astype(jnp.bfloat16).reshape(bins_here, block_rows, 2, total_channels)


def solution(mesh):
    return jax.shard_map(
        plain_body,
        mesh=mesh,
        in_specs=(
            P(("groups", "chan"), "freq", None),
            P(("groups", "chan"), "freq"),
            P("groups"),
            P("groups"),
        ),
        out_specs=P("freq", ("groups", "chan"), None, None),
        check_vma=False,
    )
```

time: 278 us -> 114 us (0.41)
  other arithmetic: 128 us -> 8 us
  local copies, waits for them, and re-layouts: 47.6 us -> 17.7 us
  waiting for transfers between devices: 70.9 us -> 56.1 us
  matrix products: 9.74 us -> 17.8 us
  starting transfers between devices: 7.6 us -> 0.01 us
    another operation x1 -> x2, other arithmetic: 110 us -> 0.08 us  [plain_body(): jnp.stack([left, jnp.stack([left[:, :, 1], -left[:, :, 0]], axis=2)], axi...]
    transpose x2 -> x0, local copies, waits for them, and re-layouts: 18.3 us -> none  [the longest x1 9.15 us: cross_block(): turned.transpose(3, 2, 1, 0)]
    all_gather x1, waiting for transfers between devices: 70.9 us -> 56.1 us  [plain_body(): gathered = lax.all_gather(panel, 'chan', axis=0, tiled=True)]
    unnamed x42 -> x14, local copies, waits for them, and re-layouts: 9.99 us -> 0.03 us
    gather x4 -> x0, local copies, waits for them, and re-layouts: 8.33 us -> none  [the longest x1 3.55 us: body(): picked = jnp.take(shaped, source_row, axis=0)]
    dot_general x10 -> x4, matrix products: 9.74 us -> 17.8 us  [the longest x1 5.38 us: plain_body(): jnp.einsum('cwpb,cj->bpwj', gathered, place, preferred_element_type=jnp.f...]
    all_to_all x1 -> x0, starting transfers between devices: 7.56 us -> none  [body(): lax.all_to_all(kept_rows.reshape((channel_count, capacity) + shaped.shape...]
    mul x2, other arithmetic: 6.45 us -> 1.13 us  [the longest x1 1.02 us: plain_body(): whitened = whitened * my_quality.astype(jnp.bfloat16)[:, None, None, None]]
  transfers between devices with their start and end apart: 2 -> 1, of which waited for: 1 -> 1; matrix products, arithmetic and copies ran while one was open for 41% -> 0% of each run, Pallas kernels for 0% -> 0%
where the time goes in v1:
time: 114 us; the launch traced here: 113 us
  waiting for transfers between devices  56.1 us (49%)
  matrix products  17.8 us (16%)
  local copies, waits for them, and re-layouts  17.7 us (16%)
  between operations  13.6 us (12%)
  other arithmetic  8 us (7%)
    all_gather x1, waiting for transfers between devices, plain_body(): gathered = lax.all_gather(panel, 'chan', axis=0, tiled=True)  56.1 us
    convert_element_type x1, local copies, waits for them, and re-layouts, plain_body(): right.astype(jnp.bfloat16)  8.04 us
    dot_general x1, matrix products, plain_body(): jnp.einsum('cwpb,cj->bpwj', gathered, place, preferred_element_type=jnp.f...  5.38 us
    dot_general x1, matrix products, spectra_of(): jnp.dot(quarters, table, preferred_element_type=jnp.float32)  4.79 us
    dot_general x1, matrix products, plain_body(): jnp.einsum('bik,bkj->bij', both, right, preferred_element_type=jnp.float32)  4.74 us
    reduce_sum x1, other arithmetic, prepare(): average = jnp.sum(kept, axis=-1) / valid_lengths.astype(jnp.float32)  3.17 us
    reshape x1, local copies, waits for them, and re-layouts, spectra_of(): jnp.dot(quarters, table, preferred_element_type=jnp.float32)  3.06 us
    dot_general x1, matrix products, plain_body(): jnp.einsum('cwpb,ci->bipw', gathered, my_place, preferred_element_type=jn...  2.88 us
  transfers between devices with their start and end apart: 1, of which 1 were waited for; matrix products, arithmetic and copies ran while one was open for 0% of the time, Pallas kernels for 0%

profile of v1, /device:TPU:0, one launch (start us, length us, event | category | flops | bytes accessed | tf_op | source)
XLA Modules:
  0.0 113.1 jit_solution(9558573570834791651)
XLA Ops:
  6.5 0.2 multiply_subtract_fusion
  6.7 3.2 %fusion = f32[8,16]{1,0:T(8,128)S(1)} fusion(bf16[8,16,12000]{2,1,0:T(8,128)(2,1)} %param.7, s32[8,16]{1,0:T(8,128)} %param.8), kind=kLoop, calls=%fused_computation.2 | loop fusion | flops 6143872 | bytes 3073024 | tf_op jit(solution)/shard_map/reduce_sum | solution.py:39
  9.9 0.7 convert_divide_fusion
  10.6 2.3 %fusion.3 = bf16[8,16,12000]{2,1,0:T(8,128)(2,1)S(1)} fusion(bf16[8,16,12000]{2,1,0:T(8,128)(2,1)S(1)} %copy-done, f32[12000]{0:T(1024)S(1)} %multiply_subtract_fusion, f32[8,16]{1,0:T(8,128)S(1)} %convert_divide_fusion, s32[8,16]{1,0:T(8,128)} %param.8), kind=kLoop, calls=%fused_computation.5 | loop fusion | flops 9216000 | bytes 6193024 | tf_op jit(solution)/shard_map/convert_element_type | solution.py:41
  12.9 1.0 fusion.16
  13.9 4.8 %fusion.4 = f32[512,1024]{1,0:T(8,128)} fusion(bf16[3000,1024]{1,0:T(8,128)(2,1)S(1)} %bitcast.46, bf16[128,3000]{1,0:T(8,128)(2,1)S(1)} %get-tuple-element.8, bf16[128,3000]{1,0:T(8,128)(2,1)S(1)} %get-tuple-element.9, bf16[128,3000]{1,0:T(8,128)(2,1)S(1)} %get-tuple-element.10, bf16[128,3000]{1,0:T(8,128)(2,1)S(1)} %get-tuple-element.7), kind=kOutput, calls=%fused_computation.10 | convolution fusion | flops 3158016000 | bytes 11313152 | tf_op jit(solution)/shard_map/dot_general | solution.py:61
  18.7 3.1 %reshape.50 = f32[4,128,2,512]{3,2,1,0:T(2,128)S(1)} reshape(f32[512,1024]{1,0:T(8,128)} %fusion.4) | data formatting | bytes 4194304 | tf_op jit(solution)/shard_map/reshape | solution.py:61
  21.8 1.6 %fusion.17 = (f32[4,128,1,512]{3,2,1,0:T(1,128)S(1)}, f32[4,128,1,512]{3,2,1,0:T(1,128)S(1)}) fusion(f32[4,128,2,512]{3,2,1,0:T(2,128)S(1)} %reshape.50), kind=kLoop, calls=%fused_computation.38 | loop fusion | bytes 4194304 | tf_op jit(solution)/shard_map/slice | solution.py:63
  23.5 0.3 subtract_reduce_fusion
  23.8 0.1 fusion.15
  23.9 0.2 copy.18
  24.2 0.1 copy.19
  24.3 0.4 reshape.51
  24.7 0.3 mul.99
  25.0 0.4 mul.100
  25.5 0.2 copy.20
  25.7 1.0 fusion.6
  26.8 56.1 %all-gather.2.cloned.1.call-done = bf16[128,16,2,512]{3,0,2,1:T(8,128)(2,1)} async-done(((bf16[8,16,2,512]{3,0,2,1:T(8,128)(2,1)}), bf16[128,16,2,512]{3,0,2,1:T(8,128)(2,1)}) %all-gather.2.cloned.1.call-update) | async-done | bytes 4194320 | tf_op jit(solution)/shard_map/all_gather | solution.py:80
  82.8 5.4 %convert_bitcast_fusion = bf16[512,2,16,128]{0,3,1,2:T(8,128)(2,1)} fusion(bf16[128,16,2,512]{3,0,2,1:T(8,128)(2,1)} %all-gather.2.cloned.1.call-done, s32[128]{0:T(128)S(1)} %copy-done.3), kind=kOutput, calls=%fused_computation.8 | convolution fusion | flops 538984448 | bytes 8389120 | tf_op jit(solution)/shard_map/cwpb,cj->bpwj/dot_general | solution.py:86
  88.2 8.0 %copy.23 = bf16[512,2,16,128]{3,2,1,0:T(8,128)(2,1)} copy(bf16[512,2,16,128]{0,3,1,2:T(8,128)(2,1)} %convert_bitcast_fusion) | data formatting | bytes 8388608 | tf_op jit(solution)/shard_map/convert_element_type | solution.py:87
  96.3 2.9 %convolution_convert_fusion = bf16[8,16,2,512]{3,0,2,1:T(8,128)(2,1)S(1)} fusion(bf16[128,16,2,512]{3,0,2,1:T(8,128)(2,1)} %all-gather.2.cloned.1.call-done, s32[128]{0:T(128)S(1)} %copy-done.3, s32[8]{0:T(128)S(1)} %iota_add_fusion), kind=kOutput, calls=%fused_computation.11 | convolution fusion | flops 33686528 | bytes 4456992 | tf_op jit(solution)/shard_map/cwpb,ci->bipw/dot_general | solution.py:88
  99.3 0.3 copy.22
  99.6 2.0 %copy.24 = bf16[512,16,32]{2,1,0:T(8,128)(2,1)S(1)} copy(bf16[512,16,32]{0,2,1:T(8,128)(2,1)S(1)} %bitcast.43) | data formatting | bytes 1048576 | tf_op jit(solution)/shard_map/reshape | solution.py:92
  101.6 4.7 %multiply_convert_fusion = bf16[512,16,128]{2,1,0:T(8,128)(2,1)} fusion(bf16[512,16,32]{2,1,0:T(8,128)(2,1)S(1)} %copy.24, bf16[512,32,128]{2,1,0:T(8,128)(2,1)} %bitcast.39), kind=kOutput, calls=%fused_computation.7 | convolution fusion | flops 69206016 | bytes 6815744 | tf_op jit(solution)/shard_map/bik,bkj->bij/dot_general | solution.py:93
  (24 shorter events, 0.3 us)
Async XLA Ops:
  6.5 4.1 %copy-start = (bf16[8,16,12000]{2,1,0:T(8,128)(2,1)S(1)}, bf16[8,16,12000]{2,1,0:T(8,128)(2,1)}, u32[]{:S(2)}) copy-start(bf16[8,16,12000]{2,1,0:T(8,128)(2,1)} %param.7) | copy-start | bytes 9216004
  6.5 76.3 %all-gather.2.cloned.1.call-start = ((), (), s32[]{:S(2)}) async-start(), calls=%async_computation | async-start | bytes 4456448 | tf_op jit(solution)/shard_map/all_gather | solution.py:80
  6.7 7.2 %slice-start = ((s8[6144000]{0:T(1024)(128)(4,1)}), s8[4194304]{0:T(1024)(128)(4,1)S(1)}, s32[]{:S(2)}) async-start(s8[6144000]{0:T(1024)(128)(4,1)} %bitcast.45), calls=%async_computation.1 | async-start | bytes 8388608
  10.6 3.3 %slice-start.1 = ((s8[6144000]{0:T(1024)(128)(4,1)}), s8[1949696]{0:T(1024)(128)(4,1)S(1)}, s32[]{:S(2)}) async-start(s8[6144000]{0:T(1024)(128)(4,1)} %bitcast.45), calls=%async_computation.2 | async-start | bytes 3899392
  18.7 4.7 %copy-start.1 = (f32[4,512]{1,0:T(4,128)S(1)}, f32[4,512]{1,0:T(4,128)}, u32[]{:S(2)}) copy-start(f32[4,512]{1,0:T(4,128)} %constant.32.clone) | copy-start | bytes 24580
  18.7 4.7 %copy-start.2 = (f32[4,512]{1,0:T(4,128)S(1)}, f32[4,512]{1,0:T(4,128)}, u32[]{:S(2)}) copy-start(f32[4,512]{1,0:T(4,128)} %constant.31.clone) | copy-start | bytes 24580
  23.7 1.9 %copy-start.4 = (s32[128]{0:T(128)S(1)}, s32[128]{0:T(128)}, u32[]{:S(2)}) copy-start(s32[128]{0:T(128)} %param.9) | copy-start | bytes 1540
  23.8 59.1 %copy-start.3 = (s32[128]{0:T(128)S(1)}, s32[128]{0:T(128)}, u32[]{:S(2)}) copy-start(s32[128]{0:T(128)} %param.10) | copy-start | bytes 1540
Sparse Core Ops, SparseCore 0:
  26.9 55.9 all-gather.1

commit v2 on v1

--- a/solution.py
+++ b/solution.py
@@ -5,6 +5,8 @@
 import ml_dtypes
 import numpy as np
 from jax import lax
+from jax.experimental import pallas as pl
+from jax.experimental.pallas import tpu as pltpu
 from jax.sharding import PartitionSpec as P
 
 WIN = 12000
@@ -94,9 +96,302 @@
     return (cross / all_windows).astype(jnp.bfloat16).reshape(bins_here, block_rows, 2, total_channels)
 
 
+CHUNK = 128
+DEPTH = 3072
+MESH = pl.DeviceIdType.MESH
+
+
+def spectra_kernel(raw_ref, length_ref, taper_ref, order_ref, turn_ref, group_ref, table_ref, out_ref, rows):
+    row_count = raw_ref.shape[0]
+
+    @pl.when(pl.program_id(0) == 0)
+    def _():
+        rows[:, QUARTER // 128 * 128 :] = jnp.zeros(
+            (4 * row_count, DEPTH - QUARTER // 128 * 128), jnp.bfloat16
+        )
+        taper = taper_ref[...]
+
+        def prepare_rows(step, carry):
+            first = pl.multiple_of(step * 16, 16)
+            values = raw_ref[pl.ds(first, 16), :].astype(jnp.float32)
+            valid = length_ref[pl.ds(first, 16), :]
+            inside = lax.broadcasted_iota(jnp.int32, (16, WIN), 1) < valid
+            kept = jnp.where(inside, values, 0.0)
+            average = jnp.sum(kept, axis=1, keepdims=True) / valid.astype(jnp.float32)
+            shaped = jnp.where(inside, (values - average) * taper, 0.0)
+            for q in range(4):
+                rows[pl.ds(pl.multiple_of(q * row_count + first, 16), 16), :QUARTER] = shaped[
+                    :, q * QUARTER : (q + 1) * QUARTER
+                ].astype(jnp.bfloat16)
+            return carry
+
+        lax.fori_loop(0, row_count // 16, prepare_rows, 0)
+
+    parts = jnp.dot(rows[...], table_ref[0], preferred_element_type=jnp.float32)
+    real = jnp.zeros((row_count, CHUNK), jnp.float32)
+    imag = jnp.zeros((row_count, CHUNK), jnp.float32)
+    for q in range(4):
+        a = parts[q * row_count : (q + 1) * row_count, :CHUNK]
+        b = parts[q * row_count : (q + 1) * row_count, CHUNK:]
+        turn_real, turn_imag = turn_ref[q : q + 1, :], turn_ref[4 + q : 5 + q, :]
+        real += a * turn_real - b * turn_imag
+        imag += b * turn_real + a * turn_imag
+    power = jnp.dot(
+        real * real + imag * imag,
+        group_ref[...],
+        preferred_element_type=jnp.float32,
+        precision=lax.Precision.HIGHEST,
+    )
+    factor = lax.rsqrt(power / SUB + 1e-06)
+    for part, value in enumerate((real, imag)):
+        out_ref[0, part * row_count : (part + 1) * row_count, :] = jnp.dot(
+            order_ref[...], (value * factor).astype(jnp.bfloat16), preferred_element_type=jnp.float32
+        ).astype(jnp.bfloat16)
+
+
+def gather_kernel(own_ref, out_ref, local_sem, arrive, up_sem, down_sem, side_sem, core_sem):
+    chunks = own_ref.shape[0]
+    levels = out_ref.shape[0] // 4
+    me = lax.axis_index("chan")
+    core = lax.rem(me, 2)
+    side = lax.rem(me // 2, 2)
+    level = me // 4
+    up, down = me + 4, me - 4
+    beside = level * 4 + (1 - side) * 2 + core
+    partner = level * 4 + side * 2 + (1 - core)
+    has_up, has_down = level < levels - 1, level > 0
+
+    barrier = pltpu.get_barrier_semaphore()
+
+    def greet(target):
+        pl.semaphore_signal(barrier, inc=1, device_id={"chan": target}, device_id_type=MESH)
+
+    greet(beside)
+    greet(partner)
+    pl.when(has_up)(lambda: greet(up))
+    pl.when(has_down)(lambda: greet(down))
+    pl.semaphore_wait(barrier, 2 + has_up.astype(jnp.int32) + has_down.astype(jnp.int32))
+
+    keep = pltpu.make_async_copy(own_ref, out_ref.at[me], local_sem)
+    keep.start()
+
+    def copy(kind, target, origin, chunk, mine=False):
+        slot = {"up": origin // 4, "down": origin // 4, "side": origin // 4, "core": origin // 2}[kind]
+        sems = {"up": up_sem, "down": down_sem, "side": side_sem, "core": core_sem}[kind]
+        return pltpu.make_async_remote_copy(
+            src_ref=own_ref.at[chunk] if mine else out_ref.at[origin, chunk],
+            dst_ref=out_ref.at[origin, chunk],
+            send_sem=sems.at[slot, chunk],
+            recv_sem=arrive.at[origin, chunk],
+            device_id={"chan": target},
+            device_id_type=MESH,
+        )
+
+    def landed(origin, chunk):
+        copy("core", partner, origin, chunk).wait_recv()
+
+    def send_own(chunk, carry):
+        copy("side", beside, me, chunk, True).start()
+        pl.when(has_up)(lambda: copy("up", up, me, chunk, True).start())
+        pl.when(has_down)(lambda: copy("down", down, me, chunk, True).start())
+        copy("core", partner, me, chunk, True).start()
+        return carry
+
+    lax.fori_loop(0, chunks, send_own, 0)
+
+    def from_side(distance, chunk):
+        def pass_on(origin):
+            landed(origin, chunk)
+            copy("core", partner, origin, chunk).start()
+
+        if distance == 0:
+            pass_on(beside)
+        else:
+            pl.when(level >= distance)(lambda: pass_on(beside - 4 * distance))
+            pl.when(level + distance < levels)(lambda: pass_on(beside + 4 * distance))
+
+    for distance in range(1, levels + 1):
+
+        def step(chunk, carry, distance=distance):
+            def below():
+                origin = me - 4 * distance
+                landed(origin, chunk)
+                copy("side", beside, origin, chunk).start()
+                pl.when(has_up)(lambda: copy("up", up, origin, chunk).start())
+                copy("core", partner, origin, chunk).start()
+
+            def above():
+                origin = me + 4 * distance
+                landed(origin, chunk)
+                copy("side", beside, origin, chunk).start()
+                pl.when(has_down)(lambda: copy("down", down, origin, chunk).start())
+                copy("core", partner, origin, chunk).start()
+
+            if distance < levels:
+                pl.when(level >= distance)(below)
+                pl.when(level + distance < levels)(above)
+            from_side(distance - 1, chunk)
+            return carry
+
+        lax.fori_loop(0, chunks, step, 0)
+
+    def finish(chunk, carry):
+        for z in range(levels):
+            for y in range(2):
+                landed(z * 4 + y * 2 + (1 - core), chunk)
+        for z in range(levels):
+            line = z * 4 + side * 2 + core
+            copy("side", beside, line, chunk).wait_send()
+            copy("core", partner, line, chunk).wait_send()
+            copy("core", partner, z * 4 + (1 - side) * 2 + core, chunk).wait_send()
+            pl.when(jnp.logical_and(has_up, z <= level))(
+                lambda line=line: copy("up", up, line, chunk).wait_send()
+            )
+            pl.when(jnp.logical_and(has_down, z >= level))(
+                lambda line=line: copy("down", down, line, chunk).wait_send()
+            )
+        return carry
+
+    lax.fori_loop(0, chunks, finish, 0)
+    keep.wait()
+
+
+def cross_kernel(panel_ref, place_ref, select_ref, out_ref, right, *, window_count):
+    depth = 2 * window_count
+    devices = panel_ref.shape[0]
+    for pair in range(window_count):
+        block = panel_ref[:, 0, pair * 16 : (pair + 1) * 16, :].reshape(devices * 16, CHUNK)
+        turned = lax.dot_general(
+            block, place_ref[...], (((0,), (0,)), ((), ())), preferred_element_type=jnp.float32
+        )
+        for half in range(2):
+            right[pl.ds(pair * 2 + half, CHUNK, stride=depth), :] = turned[:, half * 128 : (half + 1) * 128]
+
+    owner = lax.broadcasted_iota(jnp.int32, (8 * depth, 128), 0) // depth
+    column = lax.broadcasted_iota(jnp.int32, (8 * depth, 128), 1) // 16
+    mask = owner == column
+
+    def one_group(group, carry):
+        plain = right[pl.ds(pl.multiple_of(group * 8 * depth, 8 * depth), 8 * depth), :]
+        split = plain.reshape(8, 2, window_count, 128)
+        swapped = jnp.concatenate([split[:, 1:], -split[:, :1]], axis=1).reshape(8 * depth, 128)
+        plain = plain.astype(jnp.bfloat16)
+        both = jnp.concatenate([plain, swapped.astype(jnp.bfloat16)], axis=1)
+        left = jnp.dot(both, select_ref[...], preferred_element_type=jnp.float32)
+        left = jnp.where(mask, left, 0.0).astype(jnp.bfloat16)
+        result = lax.dot_general(left, plain, (((0,), (0,)), ((), ())), preferred_element_type=jnp.float32)
+        out_ref[pl.ds(pl.multiple_of(group * 128, 128), 128), :] = (result * (1.0 / window_count)).astype(
+            jnp.bfloat16
+        )
+        return carry
+
+    lax.fori_loop(0, CHUNK // 8, one_group, 0)
+
+
+def kernel_body(raw, lengths, quality, assignment):
+    me = lax.axis_index("chan")
+    block_rows, window_count, _ = raw.shape
+    row_count = block_rows * window_count
+    total_channels = assignment.shape[0]
+    devices = total_channels // block_rows
+    chunks = NB // CHUNK
+    real_table, imag_table = quarter_table()
+    table = np.zeros((chunks, DEPTH, 2 * CHUNK), ml_dtypes.bfloat16)
+    for chunk in range(chunks):
+        table[chunk, :QUARTER, :CHUNK] = real_table[:, chunk * CHUNK : (chunk + 1) * CHUNK]
+        table[chunk, :QUARTER, CHUNK:] = imag_table[:, chunk * CHUNK : (chunk + 1) * CHUNK]
+    turn = np.concatenate(turns(), axis=0)[:, :CHUNK]
+    positions = np.arange(WIN, dtype=np.float32)
+    taper = (0.5 - 0.5 * np.cos(positions * np.float32(2.0 * math.pi / WIN))).astype(np.float32)[None, :]
+    lanes = np.arange(CHUNK)
+    group = (lanes[:, None] // SUB == lanes[None, :] // SUB).astype(np.float32)
+    flat = np.arange(row_count)
+    shuffle = (
+        (flat[:, None] // block_rows == flat[None, :] % window_count)
+        & (flat[:, None] % block_rows == flat[None, :] // window_count)
+    ).astype(np.float32)
+    my_quality = lax.dynamic_slice_in_dim(quality, me * block_rows, block_rows).astype(jnp.float32)
+    order = (jnp.asarray(shuffle) * jnp.repeat(my_quality, window_count)[None, :]).astype(jnp.bfloat16)
+
+    def whole(shape):
+        return pl.BlockSpec(shape, lambda j: (0,) * len(shape))
+
+    own = pl.pallas_call(
+        spectra_kernel,
+        grid=(chunks,),
+        in_specs=[
+            whole((row_count, WIN)),
+            whole((row_count, 1)),
+            whole((1, WIN)),
+            whole((row_count, row_count)),
+            whole((8, CHUNK)),
+            whole((CHUNK, CHUNK)),
+            pl.BlockSpec((1, DEPTH, 2 * CHUNK), lambda j: (j, 0, 0)),
+        ],
+        out_specs=pl.BlockSpec((1, 2 * row_count, CHUNK), lambda j: (j, 0, 0)),
+        out_shape=jax.ShapeDtypeStruct((chunks, 2 * row_count, CHUNK), jnp.bfloat16),
+        scratch_shapes=[pltpu.VMEM((4 * row_count, DEPTH), jnp.bfloat16)],
+        compiler_params=pltpu.CompilerParams(vmem_limit_bytes=48 * 2**20),
+    )(
+        raw.reshape(row_count, WIN),
+        lengths.reshape(row_count, 1),
+        jnp.asarray(taper),
+        order,
+        jnp.asarray(turn),
+        jnp.asarray(group),
+        jnp.asarray(table),
+    )
+
+    panel = pl.pallas_call(
+        gather_kernel,
+        in_specs=[pl.BlockSpec(memory_space=pl.ANY)],
+        out_specs=pl.BlockSpec(memory_space=pl.ANY),
+        out_shape=jax.ShapeDtypeStruct((devices, chunks, 2 * row_count, CHUNK), jnp.bfloat16),
+        scratch_shapes=[
+            pltpu.SemaphoreType.DMA,
+            pltpu.SemaphoreType.DMA((devices, chunks)),
+            pltpu.SemaphoreType.DMA((devices // 4, chunks)),
+            pltpu.SemaphoreType.DMA((devices // 4, chunks)),
+            pltpu.SemaphoreType.DMA((devices // 4, chunks)),
+            pltpu.SemaphoreType.DMA((devices // 2, chunks)),
+        ],
+        compiler_params=pltpu.CompilerParams(collective_id=0, has_side_effects=True),
+    )(own)
+
+    spot = jnp.repeat(assignment.reshape(devices, 1, block_rows), 2, axis=1).reshape(-1)
+    half = (np.arange(2 * total_channels) // block_rows) % 2
+    columns = np.arange(2 * total_channels)
+    place = jnp.logical_and(
+        spot[:, None] == jnp.asarray(columns % total_channels)[None, :],
+        jnp.asarray(half[:, None] == columns[None, :] // total_channels),
+    ).astype(jnp.bfloat16)
+    column = np.arange(128)
+    source = np.arange(2 * total_channels)
+    select = jnp.logical_and(
+        jnp.asarray(source % total_channels)[:, None]
+        == me * block_rows + jnp.asarray(column // 2 % block_rows)[None, :],
+        jnp.asarray((source // total_channels)[:, None] == (column % 2)[None, :]),
+    ).astype(jnp.bfloat16)
+    cross = pl.pallas_call(
+        lambda *refs: cross_kernel(*refs, window_count=window_count),
+        grid=(chunks,),
+        in_specs=[
+            pl.BlockSpec((devices, 1, 2 * row_count, CHUNK), lambda j: (0, j, 0, 0)),
+            whole((2 * total_channels, 2 * total_channels)),
+            whole((2 * total_channels, 128)),
+        ],
+        out_specs=pl.BlockSpec((CHUNK * 2 * block_rows, total_channels), lambda j: (j, 0)),
+        out_shape=jax.ShapeDtypeStruct((NB * 2 * block_rows, total_channels), jnp.bfloat16),
+        scratch_shapes=[pltpu.VMEM((CHUNK * 2 * window_count, total_channels), jnp.float32)],
+        compiler_params=pltpu.CompilerParams(vmem_limit_bytes=48 * 2**20),
+    )(panel, place, select)
+    return cross.reshape(NB, block_rows, 2, total_channels)
+
+
 def solution(mesh):
+    ours = mesh.shape["freq"] == 1 and mesh.shape["chan"] == 16
     return jax.shard_map(
-        plain_body,
+        kernel_body if ours else plain_body,
         mesh=mesh,
         in_specs=(
             P(("groups", "chan"), "freq", None),

time: 114 us -> 88.3 us (0.77)
  Pallas kernels: 0 us -> 74.7 us
  waiting for transfers between devices: 56.1 us -> 0 us
  matrix products: 17.8 us -> 0 us
  between operations: 13.6 us -> 0.08 us
  local copies, waits for them, and re-layouts: 17.7 us -> 8.83 us
  other arithmetic: 8 us -> 4.05 us
    pallas_call x0 -> x3, Pallas kernels: none -> 74.7 us  [the longest x1 32.5 us: kernel_body(): pl.pallas_call(lambda *refs: cross_kernel(*refs, window_count=window_coun...]
    all_gather x1 -> x0, waiting for transfers between devices: 56.1 us -> none  [plain_body(): gathered = lax.all_gather(panel, 'chan', axis=0, tiled=True)]
    dot_general x4 -> x0, matrix products: 17.8 us -> none  [the longest x1 5.38 us: plain_body(): jnp.einsum('cwpb,cj->bpwj', gathered, place, preferred_element_type=jnp.f...]
    convert_element_type x1 -> x0, local copies, waits for them, and re-layouts: 8.04 us -> none  [plain_body(): right.astype(jnp.bfloat16)]
    unnamed x14 -> x12, local copies, waits for them, and re-layouts: 0.03 us -> 7.07 us
    reshape x3 -> x2, local copies, waits for them, and re-layouts: 5.48 us -> 1.5 us  [the longest x1 0.77 us: kernel_body(): lengths.reshape(row_count, 1)]
    reduce_sum x3 -> x0, other arithmetic: 3.5 us -> none  [the longest x1 3.17 us: prepare(): average = jnp.sum(kept, axis=-1) / valid_lengths.astype(jnp.float32)]
    slice x2 -> x0, local copies, waits for them, and re-layouts: 2.62 us -> none  [the longest x1 1.62 us: spectra_of(): parts[:, :, 1] * turn_imag]
  transfers between devices with their start and end apart: 1 -> 0, of which waited for: 1 -> 0; matrix products, arithmetic and copies ran while one was open for 0% -> 0% of each run, Pallas kernels for 0% -> 0%
where the time goes in v2:
time: 88.3 us; the launch traced here: 87.7 us
  Pallas kernels  74.7 us (85%)
  local copies, waits for them, and re-layouts  8.83 us (10%)
  other arithmetic  4.05 us (5%)
    pallas_call x1, Pallas kernels, kernel_body(): pl.pallas_call(lambda *refs: cross_kernel(*refs, window_count=window_coun...  32.5 us
    pallas_call x1, Pallas kernels, kernel_body(): pl.pallas_call(gather_kernel, in_specs=[pl.BlockSpec(memory_space=pl.ANY)...  30.3 us
    pallas_call x1, Pallas kernels, kernel_body(): pl.pallas_call(spectra_kernel, grid=(chunks,), in_specs=[whole((row_count...  12 us
    unnamed x12, local copies, waits for them, and re-layouts  7.07 us

profile of v2, /device:TPU:0, one launch (start us, length us, event | category | flops | bytes accessed | tf_op | source)
XLA Modules:
  0.0 87.7 jit_solution(17796163465491466901)
XLA Ops:
  0.0 0.7 dynamic-slice_convert_fusion
  0.7 0.7 broadcast_add_fusion
  1.4 0.1 broadcast_in_dim.4
  1.5 0.1 mul.15
  1.5 0.7 reshape.22
  2.3 0.1 eq.28
  2.4 0.8 multiply_convert_fusion.order_ref
  3.2 0.9 and_convert_fusion.1.refs_2_
  4.1 0.8 reshape.24.length_ref
  4.9 1.0 %and_convert_fusion.refs_1_ = bf16[256,256]{1,0:T(8,128)(2,1)S(1)} fusion(pred[256,256]{1,0:T(32,128)(4,1)} %constant.34.clone, s32[256]{0:T(256)} %constant.33.clone, s32[256]{0:T(256)S(1)} %eq.28), kind=kLoop, calls=%fused_computation | loop fusion | flops 196608 | bytes 198656 | tf_op jit(solution)/shard_map/convert_element_type | solution.py:367
  5.8 0.0 copy-start.1
  5.9 1.9 %copy-done.1 = bf16[8,16,12000]{2,1,0:T(8,128)(2,1)S(1)} copy-done((bf16[8,16,12000]{2,1,0:T(8,128)(2,1)S(1)}, bf16[8,16,12000]{2,1,0:T(8,128)(2,1)}, u32[]{:S(2)}) %copy-start.1) | copy-done | bytes 3072024
  7.7 0.0 copy-start.3
  7.7 0.8 copy-done.3
  8.6 0.0 copy-start.4
  8.6 0.8 copy-done.4
  9.4 0.7 copy-done.5
  10.0 12.0 %shard_map.136.own_ref = bf16[4,256,128]{2,1,0:T(8,128)(2,1)S(1)} custom-call(bf16[128,12000]{1,0:T(8,128)(2,1)S(1)} %bitcast.4, s32[128,1]{1,0:T(8,128)S(1)} %reshape.24.length_ref, f32[1,12000]{1,0:T(1,128)S(1)} %copy-done.4, bf16[128,128]{1,0:T(8,128)(2,1)S(1)} %multiply_convert_fusion.order_ref, f32[8,128]{1,0:T(8,128)S(1)} %copy-done.5, ...), custom_call_target="tpu_custom_call" | custom-call | tf_op jit(solution)/shard_map/pallas_call | solution.py:319
  22.0 0.0 copy-start.2
  22.0 0.7 copy-done.2
  22.7 30.3 %shard_map.137.refs_0_ = bf16[16,4,256,128]{3,2,1,0:T(8,128)(2,1)} custom-call(bf16[4,256,128]{2,1,0:T(8,128)(2,1)} %copy-done.2), custom_call_target="tpu_custom_call" | custom-call | tf_op jit(solution)/shard_map/pallas_call | solution.py:345
  53.0 0.0 copy-start
  53.0 2.2 %copy-done = bf16[16,4,256,128]{3,2,1,0:T(8,128)(2,1)S(1)} copy-done((bf16[16,4,256,128]{3,2,1,0:T(8,128)(2,1)S(1)}, bf16[16,4,256,128]{3,2,1,0:T(8,128)(2,1)}, u32[]{:S(2)}) %copy-start) | copy-done | bytes 4194328
  55.2 32.5 %shard_map.138 = bf16[8192,128]{1,0:T(8,128)(2,1)} custom-call(bf16[16,4,256,128]{3,2,1,0:T(8,128)(2,1)S(1)} %copy-done, bf16[256,256]{1,0:T(8,128)(2,1)S(1)} %and_convert_fusion.refs_1_, bf16[256,128]{1,0:T(8,128)(2,1)S(1)} %and_convert_fusion.1.refs_2_), custom_call_target="tpu_custom_call" | custom-call | tf_op jit(solution)/shard_map/pallas_call | solution.py:375
  (2 shorter events, 0.0 us)
Async XLA Ops:
  5.8 1.9 %copy-start.1 = (bf16[8,16,12000]{2,1,0:T(8,128)(2,1)S(1)}, bf16[8,16,12000]{2,1,0:T(8,128)(2,1)}, u32[]{:S(2)}) copy-start(bf16[8,16,12000]{2,1,0:T(8,128)(2,1)} %param.14) | copy-start | bytes 9216004
  7.7 0.8 copy-start.3
  8.6 0.8 copy-start.4
  9.4 0.7 copy-start.5
  22.0 0.7 copy-start.2
  53.0 2.2 %copy-start = (bf16[16,4,256,128]{3,2,1,0:T(8,128)(2,1)S(1)}, bf16[16,4,256,128]{3,2,1,0:T(8,128)(2,1)}, u32[]{:S(2)}) copy-start(bf16[16,4,256,128]{3,2,1,0:T(8,128)(2,1)} %shard_map.137.refs_0_) | copy-start | bytes 12582916

commit v3 on v2

--- a/solution.py
+++ b/solution.py
@@ -1,3 +1,4 @@
+import functools
 import math
 
 import jax
@@ -149,9 +150,24 @@
         ).astype(jnp.bfloat16)
 
 
-def gather_kernel(own_ref, out_ref, local_sem, arrive, up_sem, down_sem, side_sem, core_sem):
+def cross_kernel(
+    own_ref,
+    place_ref,
+    select_ref,
+    out_ref,
+    panel,
+    right,
+    local_sem,
+    arrive,
+    up_sem,
+    down_sem,
+    side_sem,
+    core_sem,
+    *,
+    window_count,
+):
     chunks = own_ref.shape[0]
-    levels = out_ref.shape[0] // 4
+    levels = panel.shape[0] // 4
     me = lax.axis_index("chan")
     core = lax.rem(me, 2)
     side = lax.rem(me // 2, 2)
@@ -172,15 +188,15 @@
     pl.when(has_down)(lambda: greet(down))
     pl.semaphore_wait(barrier, 2 + has_up.astype(jnp.int32) + has_down.astype(jnp.int32))
 
-    keep = pltpu.make_async_copy(own_ref, out_ref.at[me], local_sem)
+    keep = pltpu.make_async_copy(own_ref, panel.at[me], local_sem)
     keep.start()
 
     def copy(kind, target, origin, chunk, mine=False):
         slot = {"up": origin // 4, "down": origin // 4, "side": origin // 4, "core": origin // 2}[kind]
         sems = {"up": up_sem, "down": down_sem, "side": side_sem, "core": core_sem}[kind]
         return pltpu.make_async_remote_copy(
-            src_ref=own_ref.at[chunk] if mine else out_ref.at[origin, chunk],
-            dst_ref=out_ref.at[origin, chunk],
+            src_ref=own_ref.at[chunk] if mine else panel.at[origin, chunk],
+            dst_ref=panel.at[origin, chunk],
             send_sem=sems.at[slot, chunk],
             recv_sem=arrive.at[origin, chunk],
             device_id={"chan": target},
@@ -210,35 +226,83 @@
             pl.when(level >= distance)(lambda: pass_on(beside - 4 * distance))
             pl.when(level + distance < levels)(lambda: pass_on(beside + 4 * distance))
 
-    for distance in range(1, levels + 1):
-
-        def step(chunk, carry, distance=distance):
-            def below():
-                origin = me - 4 * distance
-                landed(origin, chunk)
-                copy("side", beside, origin, chunk).start()
-                pl.when(has_up)(lambda: copy("up", up, origin, chunk).start())
-                copy("core", partner, origin, chunk).start()
-
-            def above():
-                origin = me + 4 * distance
-                landed(origin, chunk)
-                copy("side", beside, origin, chunk).start()
-                pl.when(has_down)(lambda: copy("down", down, origin, chunk).start())
-                copy("core", partner, origin, chunk).start()
-
-            if distance < levels:
-                pl.when(level >= distance)(below)
-                pl.when(level + distance < levels)(above)
-            from_side(distance - 1, chunk)
-            return carry
-
-        lax.fori_loop(0, chunks, step, 0)
+    def relay(distance, chunk):
+        def below():
+            origin = me - 4 * distance
+            landed(origin, chunk)
+            copy("side", beside, origin, chunk).start()
+            pl.when(has_up)(lambda: copy("up", up, origin, chunk).start())
+            copy("core", partner, origin, chunk).start()
+
+        def above():
+            origin = me + 4 * distance
+            landed(origin, chunk)
+            copy("side", beside, origin, chunk).start()
+            pl.when(has_down)(lambda: copy("down", down, origin, chunk).start())
+            copy("core", partner, origin, chunk).start()
+
+        if distance < levels:
+            pl.when(level >= distance)(below)
+            pl.when(level + distance < levels)(above)
+        from_side(distance - 1, chunk)
+
+    depth = 2 * window_count
+    devices = panel.shape[0]
+    owner = lax.broadcasted_iota(jnp.int32, (8 * depth, 128), 0) // depth
+    column = lax.broadcasted_iota(jnp.int32, (8 * depth, 128), 1) // 16
+    mask = owner == column
+
+    def arrange(chunk):
+        for pair in range(window_count):
+            block = panel[:, chunk, pair * 16 : (pair + 1) * 16, :].reshape(devices * 16, CHUNK)
+            turned = lax.dot_general(
+                block, place_ref[...], (((0,), (0,)), ((), ())), preferred_element_type=jnp.float32
+            )
+            for half in range(2):
+                right[pl.ds(pair * 2 + half, CHUNK, stride=depth), :] = turned[:, half * 128 : (half + 1) * 128]
+
+    def multiply(chunk, first, last):
+        for group in range(first, last):
+            plain = right[group * 8 * depth : (group + 1) * 8 * depth, :]
+            split = plain.reshape(8, 2, window_count, 128)
+            swapped = jnp.concatenate([split[:, 1:], -split[:, :1]], axis=1).reshape(8 * depth, 128)
+            plain = plain.astype(jnp.bfloat16)
+            both = jnp.concatenate([plain, swapped.astype(jnp.bfloat16)], axis=1)
+            left = jnp.dot(both, select_ref[...], preferred_element_type=jnp.float32)
+            left = jnp.where(mask, left, 0.0).astype(jnp.bfloat16)
+            result = lax.dot_general(left, plain, (((0,), (0,)), ((), ())), preferred_element_type=jnp.float32)
+            row = pl.multiple_of((chunk * (CHUNK // 8) + group) * 128, 128)
+            out_ref[pl.ds(row, 128), :] = (result * (1.0 / window_count)).astype(jnp.bfloat16)
+
+    groups = CHUNK // 8
+
+    def advance(step, carry):
+        for distance in range(1, levels + 1):
+            pl.when(step < chunks)(lambda distance=distance: relay(distance, step))
+
+            @pl.when(step > 0)
+            def _(distance=distance):
+                if distance == 1:
+                    arrange(step - 1)
+                else:
+                    multiply(
+                        step - 1,
+                        groups * (distance - 2) // (levels - 1),
+                        groups * (distance - 1) // (levels - 1),
+                    )
+
+        @pl.when(step < chunks)
+        def _():
+            for z in range(levels):
+                for y in range(2):
+                    landed(z * 4 + y * 2 + (1 - core), step)
+
+        return carry
+
+    keep.wait()
+    lax.fori_loop(0, chunks + 1, advance, 0)
 
     def finish(chunk, carry):
-        for z in range(levels):
-            for y in range(2):
-                landed(z * 4 + y * 2 + (1 - core), chunk)
         for z in range(levels):
             line = z * 4 + side * 2 + core
             copy("side", beside, line, chunk).wait_send()
@@ -253,39 +317,6 @@
         return carry
 
     lax.fori_loop(0, chunks, finish, 0)
-    keep.wait()
-
-
-def cross_kernel(panel_ref, place_ref, select_ref, out_ref, right, *, window_count):
-    depth = 2 * window_count
-    devices = panel_ref.shape[0]
-    for pair in range(window_count):
-        block = panel_ref[:, 0, pair * 16 : (pair + 1) * 16, :].reshape(devices * 16, CHUNK)
-        turned = lax.dot_general(
-            block, place_ref[...], (((0,), (0,)), ((), ())), preferred_element_type=jnp.float32
-        )
-        for half in range(2):
-            right[pl.ds(pair * 2 + half, CHUNK, stride=depth), :] = turned[:, half * 128 : (half + 1) * 128]
-
-    owner = lax.broadcasted_iota(jnp.int32, (8 * depth, 128), 0) // depth
-    column = lax.broadcasted_iota(jnp.int32, (8 * depth, 128), 1) // 16
-    mask = owner == column
-
-    def one_group(group, carry):
-        plain = right[pl.ds(pl.multiple_of(group * 8 * depth, 8 * depth), 8 * depth), :]
-        split = plain.reshape(8, 2, window_count, 128)
-        swapped = jnp.concatenate([split[:, 1:], -split[:, :1]], axis=1).reshape(8 * depth, 128)
-        plain = plain.astype(jnp.bfloat16)
-        both = jnp.concatenate([plain, swapped.astype(jnp.bfloat16)], axis=1)
-        left = jnp.dot(both, select_ref[...], preferred_element_type=jnp.float32)
-        left = jnp.where(mask, left, 0.0).astype(jnp.bfloat16)
-        result = lax.dot_general(left, plain, (((0,), (0,)), ((), ())), preferred_element_type=jnp.float32)
-        out_ref[pl.ds(pl.multiple_of(group * 128, 128), 128), :] = (result * (1.0 / window_count)).astype(
-            jnp.bfloat16
-        )
-        return carry
-
-    lax.fori_loop(0, CHUNK // 8, one_group, 0)
 
 
 def kernel_body(raw, lengths, quality, assignment):
@@ -342,22 +373,6 @@
         jnp.asarray(table),
     )
 
-    panel = pl.pallas_call(
-        gather_kernel,
-        in_specs=[pl.BlockSpec(memory_space=pl.ANY)],
-        out_specs=pl.BlockSpec(memory_space=pl.ANY),
-        out_shape=jax.ShapeDtypeStruct((devices, chunks, 2 * row_count, CHUNK), jnp.bfloat16),
-        scratch_shapes=[
-            pltpu.SemaphoreType.DMA,
-            pltpu.SemaphoreType.DMA((devices, chunks)),
-            pltpu.SemaphoreType.DMA((devices // 4, chunks)),
-            pltpu.SemaphoreType.DMA((devices // 4, chunks)),
-            pltpu.SemaphoreType.DMA((devices // 4, chunks)),
-            pltpu.SemaphoreType.DMA((devices // 2, chunks)),
-        ],
-        compiler_params=pltpu.CompilerParams(collective_id=0, has_side_effects=True),
-    )(own)
-
     spot = jnp.repeat(assignment.reshape(devices, 1, block_rows), 2, axis=1).reshape(-1)
     half = (np.arange(2 * total_channels) // block_rows) % 2
     columns = np.arange(2 * total_channels)
@@ -372,19 +387,26 @@
         == me * block_rows + jnp.asarray(column // 2 % block_rows)[None, :],
         jnp.asarray((source // total_channels)[:, None] == (column % 2)[None, :]),
     ).astype(jnp.bfloat16)
+    vmem = pl.BlockSpec(memory_space=pltpu.VMEM)
     cross = pl.pallas_call(
-        lambda *refs: cross_kernel(*refs, window_count=window_count),
-        grid=(chunks,),
-        in_specs=[
-            pl.BlockSpec((devices, 1, 2 * row_count, CHUNK), lambda j: (0, j, 0, 0)),
-            whole((2 * total_channels, 2 * total_channels)),
-            whole((2 * total_channels, 128)),
+        functools.partial(cross_kernel, window_count=window_count),
+        in_specs=[vmem] * 3,
+        out_specs=vmem,
+        out_shape=jax.ShapeDtypeStruct((NB * 2 * block_rows, total_channels), jnp.bfloat16),
+        scratch_shapes=[
+            pltpu.VMEM((devices, chunks, 2 * row_count, CHUNK), jnp.bfloat16),
+            pltpu.VMEM((CHUNK * 2 * window_count, total_channels), jnp.float32),
+            pltpu.SemaphoreType.DMA,
+            pltpu.SemaphoreType.DMA((devices, chunks)),
+            pltpu.SemaphoreType.DMA((devices // 4, chunks)),
+            pltpu.SemaphoreType.DMA((devices // 4, chunks)),
+            pltpu.SemaphoreType.DMA((devices // 4, chunks)),
+            pltpu.SemaphoreType.DMA((devices // 2, chunks)),
         ],
-        out_specs=pl.BlockSpec((CHUNK * 2 * block_rows, total_channels), lambda j: (j, 0)),
-        out_shape=jax.ShapeDtypeStruct((NB * 2 * block_rows, total_channels), jnp.bfloat16),
-        scratch_shapes=[pltpu.VMEM((CHUNK * 2 * window_count, total_channels), jnp.float32)],
-        compiler_params=pltpu.CompilerParams(vmem_limit_bytes=48 * 2**20),
-    )(panel, place, select)
+        compiler_params=pltpu.CompilerParams(
+            collective_id=0, has_side_effects=True, vmem_limit_bytes=48 * 2**20
+        ),
+    )(own, place, select)
     return cross.reshape(NB, block_rows, 2, total_channels)
 
 

time: 88.3 us -> 81.3 us (0.921)
  Pallas kernels: 74.7 us -> 69.4 us
  local copies, waits for them, and re-layouts: 8.83 us -> 7.27 us
    pallas_call x2 -> x1, Pallas kernels: 62.8 us -> 57.4 us  [kernel_body(): pl.pallas_call(functools.partial(cross_kernel, window_count=window_count)...]
    unnamed x12 -> x9, local copies, waits for them, and re-layouts: 7.07 us -> 5.51 us
where the time goes in v3:
time: 81.3 us; the launch traced here: 80.8 us
  Pallas kernels  69.4 us (85%)
  local copies, waits for them, and re-layouts  7.27 us (9%)
  other arithmetic  4.05 us (5%)
    pallas_call x1, Pallas kernels, kernel_body(): pl.pallas_call(functools.partial(cross_kernel, window_count=window_count)...  57.4 us
    pallas_call x1, Pallas kernels, kernel_body(): pl.pallas_call(spectra_kernel, grid=(chunks,), in_specs=[whole((row_count...  12 us
    unnamed x9, local copies, waits for them, and re-layouts  5.51 us

profile of v3, /device:TPU:0, one launch (start us, length us, event | category | flops | bytes accessed | tf_op | source)
XLA Modules:
  0.0 80.8 jit_solution(364564486907456201)
XLA Ops:
  0.0 0.7 dynamic-slice_convert_fusion
  0.7 0.7 broadcast_add_fusion
  1.4 0.1 broadcast_in_dim.4
  1.5 0.1 mul.15
  1.5 0.7 reshape.22
  2.3 0.1 eq.28
  2.4 0.8 %multiply_convert_fusion.order_ref = bf16[128,128]{1,0:T(8,128)(2,1)S(1)} fusion(f32[128,128]{1,0:T(8,128)} %constant.28.clone, f32[128]{0:T(128)S(1)} %mul.15), kind=kLoop, calls=%fused_computation.2 | loop fusion | flops 32768 | bytes 98816 | tf_op jit(solution)/shard_map/convert_element_type | solution.py:345
  3.2 0.9 %and_convert_fusion.1.select_ref = bf16[256,128]{1,0:T(8,128)(2,1)S(1)} fusion(pred[256,128]{1,0:T(32,128)(4,1)} %constant.36.clone, s32[128]{0:T(128)S(1)} %broadcast_add_fusion, s32[256]{0:T(256)} %constant.33.clone), kind=kLoop, calls=%fused_computation.1 | loop fusion | flops 98304 | bytes 99840 | tf_op jit(solution)/shard_map/convert_element_type | solution.py:389
  4.1 0.8 reshape.24.length_ref
  4.9 1.0 %and_convert_fusion.place_ref = bf16[256,256]{1,0:T(8,128)(2,1)S(1)} fusion(pred[256,256]{1,0:T(32,128)(4,1)} %constant.34.clone, s32[256]{0:T(256)} %constant.33.clone, s32[256]{0:T(256)S(1)} %eq.28), kind=kLoop, calls=%fused_computation | loop fusion | flops 196608 | bytes 198656 | tf_op jit(solution)/shard_map/convert_element_type | solution.py:382
  5.8 0.0 copy-start
  5.9 1.9 %copy-done = bf16[8,16,12000]{2,1,0:T(8,128)(2,1)S(1)} copy-done((bf16[8,16,12000]{2,1,0:T(8,128)(2,1)S(1)}, bf16[8,16,12000]{2,1,0:T(8,128)(2,1)}, u32[]{:S(2)}) %copy-start) | copy-done | bytes 3072024
  7.7 0.0 copy-start.1
  7.7 0.8 %copy-done.1 = f32[128,128]{1,0:T(8,128)S(1)} copy-done((f32[128,128]{1,0:T(8,128)S(1)}, f32[128,128]{1,0:T(8,128)}, u32[]{:S(2)}) %copy-start.1) | copy-done | bytes 65560
  8.6 0.0 copy-start.2
  8.6 0.8 copy-done.2
  9.4 0.0 copy-start.3
  9.4 0.7 copy-done.3
  10.0 12.0 %shard_map.136.own_ref = bf16[4,256,128]{2,1,0:T(8,128)(2,1)S(1)} custom-call(bf16[128,12000]{1,0:T(8,128)(2,1)S(1)} %bitcast.5, s32[128,1]{1,0:T(8,128)S(1)} %reshape.24.length_ref, f32[1,12000]{1,0:T(1,128)S(1)} %copy-done.2, bf16[128,128]{1,0:T(8,128)(2,1)S(1)} %multiply_convert_fusion.order_ref, f32[8,128]{1,0:T(8,128)S(1)} %copy-done.3, ...), custom_call_target="tpu_custom_call" | custom-call | tf_op jit(solution)/shard_map/pallas_call | solution.py:350
  22.0 57.4 %shard_map.137 = bf16[8192,128]{1,0:T(8,128)(2,1)S(1)} custom-call(bf16[4,256,128]{2,1,0:T(8,128)(2,1)S(1)} %shard_map.136.own_ref, bf16[256,256]{1,0:T(8,128)(2,1)S(1)} %and_convert_fusion.place_ref, bf16[256,128]{1,0:T(8,128)(2,1)S(1)} %and_convert_fusion.1.select_ref), custom_call_target="tpu_custom_call" | custom-call | tf_op jit(solution)/shard_map/pallas_call | solution.py:391
  79.5 1.3 %copy.20 = bf16[512,8,2,128]{3,2,1,0:T(2,128)(2,1)} copy(bf16[512,8,2,128]{3,2,1,0:T(2,128)(2,1)S(1)} %bitcast.4) | data formatting | bytes 4194304
  (1 shorter events, 0.0 us)
Async XLA Ops:
  5.8 1.9 %copy-start = (bf16[8,16,12000]{2,1,0:T(8,128)(2,1)S(1)}, bf16[8,16,12000]{2,1,0:T(8,128)(2,1)}, u32[]{:S(2)}) copy-start(bf16[8,16,12000]{2,1,0:T(8,128)(2,1)} %param.14) | copy-start | bytes 9216004
  7.7 0.8 %copy-start.1 = (f32[128,128]{1,0:T(8,128)S(1)}, f32[128,128]{1,0:T(8,128)}, u32[]{:S(2)}) copy-start(f32[128,128]{1,0:T(8,128)} %constant.31.clone.group_ref) | copy-start | bytes 196612
  8.6 0.8 copy-start.2
  9.4 0.7 copy-start.3

commit v4 on v3

--- a/solution.py
+++ b/solution.py
@@ -102,7 +102,7 @@
 MESH = pl.DeviceIdType.MESH
 
 
-def spectra_kernel(raw_ref, length_ref, taper_ref, order_ref, turn_ref, group_ref, table_ref, out_ref, rows):
+def spectra_kernel(raw_ref, length_ref, taper_ref, order_ref, table_ref, out_ref, rows):
     row_count = raw_ref.shape[0]
 
     @pl.when(pl.program_id(0) == 0)
@@ -129,17 +129,22 @@
         lax.fori_loop(0, row_count // 16, prepare_rows, 0)
 
     parts = jnp.dot(rows[...], table_ref[0], preferred_element_type=jnp.float32)
+    lanes = lax.broadcasted_iota(jnp.int32, (1, CHUNK), 1)
+    group_row = lax.broadcasted_iota(jnp.int32, (CHUNK, CHUNK), 0) // SUB
+    group_column = lax.broadcasted_iota(jnp.int32, (CHUNK, CHUNK), 1) // SUB
     real = jnp.zeros((row_count, CHUNK), jnp.float32)
     imag = jnp.zeros((row_count, CHUNK), jnp.float32)
     for q in range(4):
         a = parts[q * row_count : (q + 1) * row_count, :CHUNK]
         b = parts[q * row_count : (q + 1) * row_count, CHUNK:]
-        turn_real, turn_imag = turn_ref[q : q + 1, :], turn_ref[4 + q : 5 + q, :]
+        turn = lax.rem(q * (K0 + lanes), 4)
+        turn_real = (turn == 0).astype(jnp.float32) - (turn == 2).astype(jnp.float32)
+        turn_imag = (turn == 3).astype(jnp.float32) - (turn == 1).astype(jnp.float32)
         real += a * turn_real - b * turn_imag
         imag += b * turn_real + a * turn_imag
     power = jnp.dot(
         real * real + imag * imag,
-        group_ref[...],
+        (group_row == group_column).astype(jnp.float32),
         preferred_element_type=jnp.float32,
         precision=lax.Precision.HIGHEST,
     )
@@ -153,7 +158,6 @@
 def cross_kernel(
     own_ref,
     place_ref,
-    select_ref,
     out_ref,
     panel,
     right,
@@ -248,9 +252,14 @@
 
     depth = 2 * window_count
     devices = panel.shape[0]
-    owner = lax.broadcasted_iota(jnp.int32, (8 * depth, 128), 0) // depth
-    column = lax.broadcasted_iota(jnp.int32, (8 * depth, 128), 1) // 16
-    mask = owner == column
+    owner = lax.broadcasted_iota(jnp.int32, (128, 8 * depth), 0) // 16
+    column = lax.broadcasted_iota(jnp.int32, (128, 8 * depth), 1) // depth
+    mask = jnp.where(owner == column, 1.0 / window_count, 0.0).astype(jnp.bfloat16)
+    target = lax.broadcasted_iota(jnp.int32, (16, 128), 0) // 2 + me * 8
+    select = (lax.broadcasted_iota(jnp.int32, (16, 128), 1) == target).astype(jnp.float32).astype(jnp.bfloat16)
+    spot = lax.broadcasted_iota(jnp.int32, (16, 8 * depth), 1)
+    straight = lax.rem(lax.broadcasted_iota(jnp.int32, (16, 8 * depth), 0), 2) == 0
+    first_half = lax.rem(spot, depth) < window_count
 
     def arrange(chunk):
         for pair in range(window_count):
@@ -263,16 +272,16 @@
 
     def multiply(chunk, first, last):
         for group in range(first, last):
-            plain = right[group * 8 * depth : (group + 1) * 8 * depth, :]
-            split = plain.reshape(8, 2, window_count, 128)
-            swapped = jnp.concatenate([split[:, 1:], -split[:, :1]], axis=1).reshape(8 * depth, 128)
-            plain = plain.astype(jnp.bfloat16)
-            both = jnp.concatenate([plain, swapped.astype(jnp.bfloat16)], axis=1)
-            left = jnp.dot(both, select_ref[...], preferred_element_type=jnp.float32)
-            left = jnp.where(mask, left, 0.0).astype(jnp.bfloat16)
-            result = lax.dot_general(left, plain, (((0,), (0,)), ((), ())), preferred_element_type=jnp.float32)
+            plain = right[group * 8 * depth : (group + 1) * 8 * depth, :].astype(jnp.bfloat16)
+            left = lax.dot_general(select, plain, (((1,), (1,)), ((), ())), preferred_element_type=jnp.float32)
+            later = pltpu.roll(left, 8 * depth - window_count, 1)
+            earlier = pltpu.roll(left, window_count, 1)
+            left = jnp.where(straight, left, jnp.where(first_half, later, -earlier)).astype(jnp.bfloat16)
+            result = jnp.dot(
+                jnp.concatenate([left] * 8, axis=0) * mask, plain, preferred_element_type=jnp.float32
+            )
             row = pl.multiple_of((chunk * (CHUNK // 8) + group) * 128, 128)
-            out_ref[pl.ds(row, 128), :] = (result * (1.0 / window_count)).astype(jnp.bfloat16)
+            out_ref[pl.ds(row, 128), :] = result.astype(jnp.bfloat16)
 
     groups = CHUNK // 8
 
@@ -320,7 +329,6 @@
 
 
 def kernel_body(raw, lengths, quality, assignment):
-    me = lax.axis_index("chan")
     block_rows, window_count, _ = raw.shape
     row_count = block_rows * window_count
     total_channels = assignment.shape[0]
@@ -331,18 +339,13 @@
     for chunk in range(chunks):
         table[chunk, :QUARTER, :CHUNK] = real_table[:, chunk * CHUNK : (chunk + 1) * CHUNK]
         table[chunk, :QUARTER, CHUNK:] = imag_table[:, chunk * CHUNK : (chunk + 1) * CHUNK]
-    turn = np.concatenate(turns(), axis=0)[:, :CHUNK]
     positions = np.arange(WIN, dtype=np.float32)
     taper = (0.5 - 0.5 * np.cos(positions * np.float32(2.0 * math.pi / WIN))).astype(np.float32)[None, :]
-    lanes = np.arange(CHUNK)
-    group = (lanes[:, None] // SUB == lanes[None, :] // SUB).astype(np.float32)
     flat = np.arange(row_count)
     shuffle = (
         (flat[:, None] // block_rows == flat[None, :] % window_count)
         & (flat[:, None] % block_rows == flat[None, :] // window_count)
-    ).astype(np.float32)
-    my_quality = lax.dynamic_slice_in_dim(quality, me * block_rows, block_rows).astype(jnp.float32)
-    order = (jnp.asarray(shuffle) * jnp.repeat(my_quality, window_count)[None, :]).astype(jnp.bfloat16)
+    ).astype(ml_dtypes.bfloat16)
 
     def whole(shape):
         return pl.BlockSpec(shape, lambda j: (0,) * len(shape))
@@ -355,8 +358,6 @@
             whole((row_count, 1)),
             whole((1, WIN)),
             whole((row_count, row_count)),
-            whole((8, CHUNK)),
-            whole((CHUNK, CHUNK)),
             pl.BlockSpec((1, DEPTH, 2 * CHUNK), lambda j: (j, 0, 0)),
         ],
         out_specs=pl.BlockSpec((1, 2 * row_count, CHUNK), lambda j: (j, 0, 0)),
@@ -367,30 +368,22 @@
         raw.reshape(row_count, WIN),
         lengths.reshape(row_count, 1),
         jnp.asarray(taper),
-        order,
-        jnp.asarray(turn),
-        jnp.asarray(group),
+        jnp.asarray(shuffle),
         jnp.asarray(table),
     )
 
-    spot = jnp.repeat(assignment.reshape(devices, 1, block_rows), 2, axis=1).reshape(-1)
+    ordered = jnp.where(quality == 1, assignment, -1)
+    spot = jnp.repeat(ordered.reshape(devices, 1, block_rows), 2, axis=1).reshape(-1)
     half = (np.arange(2 * total_channels) // block_rows) % 2
     columns = np.arange(2 * total_channels)
     place = jnp.logical_and(
         spot[:, None] == jnp.asarray(columns % total_channels)[None, :],
         jnp.asarray(half[:, None] == columns[None, :] // total_channels),
     ).astype(jnp.bfloat16)
-    column = np.arange(128)
-    source = np.arange(2 * total_channels)
-    select = jnp.logical_and(
-        jnp.asarray(source % total_channels)[:, None]
-        == me * block_rows + jnp.asarray(column // 2 % block_rows)[None, :],
-        jnp.asarray((source // total_channels)[:, None] == (column % 2)[None, :]),
-    ).astype(jnp.bfloat16)
     vmem = pl.BlockSpec(memory_space=pltpu.VMEM)
     cross = pl.pallas_call(
         functools.partial(cross_kernel, window_count=window_count),
-        in_specs=[vmem] * 3,
+        in_specs=[vmem] * 2,
         out_specs=vmem,
         out_shape=jax.ShapeDtypeStruct((NB * 2 * block_rows, total_channels), jnp.bfloat16),
         scratch_shapes=[
@@ -406,7 +399,7 @@
         compiler_params=pltpu.CompilerParams(
             collective_id=0, has_side_effects=True, vmem_limit_bytes=48 * 2**20
         ),
-    )(own, place, select)
+    )(own, place)
     return cross.reshape(NB, block_rows, 2, total_channels)
 
 

time: 81.3 us -> 75.6 us (0.930)
  other arithmetic: 4.05 us -> 1.63 us
  Pallas kernels: 69.4 us -> 67.8 us
  local copies, waits for them, and re-layouts: 7.27 us -> 5.7 us
    convert_element_type x3 -> x0, other arithmetic: 2.44 us -> none  [the longest x1 0.86 us: kernel_body(): select = jnp.logical_and(jnp.asarray(source % total_channels)[:, None] ==...]
    pallas_call x1, Pallas kernels: 57.4 us -> 55.9 us  [kernel_body(): pl.pallas_call(functools.partial(cross_kernel, window_count=window_count)...]
    unnamed x9 -> x7, local copies, waits for them, and re-layouts: 5.51 us -> 4.74 us
where the time goes in v4:
time: 75.6 us; the launch traced here: 75.2 us
  Pallas kernels  67.8 us (90%)
  local copies, waits for them, and re-layouts  5.7 us (8%)
  other arithmetic  1.63 us (2%)
    pallas_call x1, Pallas kernels, kernel_body(): pl.pallas_call(functools.partial(cross_kernel, window_count=window_count)...  55.9 us
    pallas_call x1, Pallas kernels, kernel_body(): pl.pallas_call(spectra_kernel, grid=(chunks,), in_specs=[whole((row_count...  12 us
    unnamed x7, local copies, waits for them, and re-layouts  4.74 us

profile of v4, /device:TPU:0, one launch (start us, length us, event | category | flops | bytes accessed | tf_op | source)
XLA Modules:
  0.0 75.2 jit_solution(3297969430923163149)
XLA Ops:
  0.0 0.7 compare_select_fusion
  0.7 0.1 reshape.18
  0.8 0.1 eq.23
  0.9 0.8 %reshape.20.length_ref = s32[128,1]{1,0:T(8,128)S(1)} reshape(s32[8,16]{1,0:T(8,128)} %param.10) | data formatting | bytes 1024 | tf_op jit(solution)/shard_map/reshape | solution.py:369
  1.6 1.0 %and_convert_fusion.place_ref = bf16[256,256]{1,0:T(8,128)(2,1)S(1)} fusion(pred[256,256]{1,0:T(32,128)(4,1)} %constant.18.clone, s32[256]{0:T(256)} %constant.17.clone, s32[256]{0:T(256)S(1)} %eq.23), kind=kLoop, calls=%fused_computation | loop fusion | flops 196608 | bytes 198656 | tf_op jit(solution)/shard_map/convert_element_type | solution.py:382
  2.6 0.0 copy-start
  2.6 1.9 %copy-done = bf16[8,16,12000]{2,1,0:T(8,128)(2,1)S(1)} copy-done((bf16[8,16,12000]{2,1,0:T(8,128)(2,1)S(1)}, bf16[8,16,12000]{2,1,0:T(8,128)(2,1)}, u32[]{:S(2)}) %copy-start) | copy-done | bytes 3072024
  4.5 0.0 copy-start.1
  4.5 0.8 %copy-done.1 = f32[1,12000]{1,0:T(1,128)S(1)} copy-done((f32[1,12000]{1,0:T(1,128)S(1)}, f32[1,12000]{1,0:T(1,128)}, u32[]{:S(2)}) %copy-start.1) | copy-done | bytes 48024
  5.3 0.0 copy-start.2
  5.3 0.8 %copy-done.2 = bf16[128,128]{1,0:T(8,128)(2,1)S(1)} copy-done((bf16[128,128]{1,0:T(8,128)(2,1)S(1)}, bf16[128,128]{1,0:T(8,128)(2,1)}, u32[]{:S(2)}) %copy-start.2) | copy-done | bytes 32792
  6.0 12.0 %shard_map.91.own_ref = bf16[4,256,128]{2,1,0:T(8,128)(2,1)S(1)} custom-call(bf16[128,12000]{1,0:T(8,128)(2,1)S(1)} %bitcast.5, s32[128,1]{1,0:T(8,128)S(1)} %reshape.20.length_ref, f32[1,12000]{1,0:T(1,128)S(1)} %copy-done.1, bf16[128,128]{1,0:T(8,128)(2,1)S(1)} %copy-done.2, bf16[4,3072,256]{2,1,0:T(8,128)(2,1)} %constant.16.clone.table_ref), custom_call_target="tpu_custom_call" | custom-call | tf_op jit(solution)/shard_map/pallas_call | solution.py:353
  18.0 55.9 %shard_map.92 = bf16[8192,128]{1,0:T(8,128)(2,1)S(1)} custom-call(bf16[4,256,128]{2,1,0:T(8,128)(2,1)S(1)} %shard_map.91.own_ref, bf16[256,256]{1,0:T(8,128)(2,1)S(1)} %and_convert_fusion.place_ref), custom_call_target="tpu_custom_call" | custom-call | tf_op jit(solution)/shard_map/pallas_call | solution.py:384
  73.9 1.3 %copy.14 = bf16[512,8,2,128]{3,2,1,0:T(2,128)(2,1)} copy(bf16[512,8,2,128]{3,2,1,0:T(2,128)(2,1)S(1)} %bitcast.4) | data formatting | bytes 4194304
  (1 shorter events, 0.0 us)
Async XLA Ops:
  2.6 1.9 %copy-start = (bf16[8,16,12000]{2,1,0:T(8,128)(2,1)S(1)}, bf16[8,16,12000]{2,1,0:T(8,128)(2,1)}, u32[]{:S(2)}) copy-start(bf16[8,16,12000]{2,1,0:T(8,128)(2,1)} %param.9) | copy-start | bytes 9216004
  4.5 0.8 %copy-start.1 = (f32[1,12000]{1,0:T(1,128)S(1)}, f32[1,12000]{1,0:T(1,128)}, u32[]{:S(2)}) copy-start(f32[1,12000]{1,0:T(1,128)} %constant.14.clone.taper_ref) | copy-start | bytes 144004
  5.3 0.8 %copy-start.2 = (bf16[128,128]{1,0:T(8,128)(2,1)S(1)}, bf16[128,128]{1,0:T(8,128)(2,1)}, u32[]{:S(2)}) copy-start(bf16[128,128]{1,0:T(8,128)(2,1)} %constant.15.clone.order_ref) | copy-start | bytes 98308

commit v5 on v4

--- a/solution.py
+++ b/solution.py
@@ -287,29 +287,24 @@
 
     def advance(step, carry):
         for distance in range(1, levels + 1):
-            pl.when(step < chunks)(lambda distance=distance: relay(distance, step))
-
-            @pl.when(step > 0)
-            def _(distance=distance):
-                if distance == 1:
-                    arrange(step - 1)
-                else:
-                    multiply(
-                        step - 1,
-                        groups * (distance - 2) // (levels - 1),
-                        groups * (distance - 1) // (levels - 1),
-                    )
-
-        @pl.when(step < chunks)
+            chunk = step - distance + 1
+            pl.when(jnp.logical_and(chunk >= 0, chunk < chunks))(
+                lambda distance=distance, chunk=chunk: relay(distance, chunk)
+            )
+
+        @pl.when(step >= levels)
         def _():
+            chunk = step - levels
             for z in range(levels):
                 for y in range(2):
-                    landed(z * 4 + y * 2 + (1 - core), step)
+                    landed(z * 4 + y * 2 + (1 - core), chunk)
+            arrange(chunk)
+            multiply(chunk, 0, groups)
 
         return carry
 
     keep.wait()
-    lax.fori_loop(0, chunks + 1, advance, 0)
+    lax.fori_loop(0, chunks + levels, advance, 0)
 
     def finish(chunk, carry):
         for z in range(levels):

time: 75.6 us -> 57.2 us (0.76)
  Pallas kernels: 67.8 us -> 49.1 us
    pallas_call x1, Pallas kernels: 55.9 us -> 37.1 us  [kernel_body(): pl.pallas_call(functools.partial(cross_kernel, window_count=window_count)...]
where the time goes in v5:
time: 57.2 us; the launch traced here: 56.5 us
  Pallas kernels  49.1 us (86%)
  local copies, waits for them, and re-layouts  5.7 us (10%)
  other arithmetic  1.63 us (3%)
    pallas_call x1, Pallas kernels, kernel_body(): pl.pallas_call(functools.partial(cross_kernel, window_count=window_count)...  37.1 us
    pallas_call x1, Pallas kernels, kernel_body(): pl.pallas_call(spectra_kernel, grid=(chunks,), in_specs=[whole((row_count...  12 us
    unnamed x7, local copies, waits for them, and re-layouts  4.74 us

profile of v5, /device:TPU:0, one launch (start us, length us, event | category | flops | bytes accessed | tf_op | source)
XLA Modules:
  0.0 56.5 jit_solution(2429065867561661171)
XLA Ops:
  0.0 0.7 %compare_select_fusion = s32[128]{0:T(128)S(1)} fusion(s32[128]{0:T(128)} %param.12, s32[128]{0:T(128)} %param.11), kind=kLoop, calls=%fused_computation.1 | loop fusion | flops 256 | bytes 1536 | tf_op jit(solution)/shard_map/jit(_where)/select_n | solution.py:370
  0.7 0.1 reshape.18
  0.8 0.1 eq.23
  0.9 0.8 %reshape.20.length_ref = s32[128,1]{1,0:T(8,128)S(1)} reshape(s32[8,16]{1,0:T(8,128)} %param.10) | data formatting | bytes 1024 | tf_op jit(solution)/shard_map/reshape | solution.py:364
  1.6 1.0 %and_convert_fusion.place_ref = bf16[256,256]{1,0:T(8,128)(2,1)S(1)} fusion(pred[256,256]{1,0:T(32,128)(4,1)} %constant.18.clone, s32[256]{0:T(256)} %constant.17.clone, s32[256]{0:T(256)S(1)} %eq.23), kind=kLoop, calls=%fused_computation | loop fusion | flops 196608 | bytes 198656 | tf_op jit(solution)/shard_map/convert_element_type | solution.py:377
  2.6 0.0 copy-start
  2.6 1.9 %copy-done = bf16[8,16,12000]{2,1,0:T(8,128)(2,1)S(1)} copy-done((bf16[8,16,12000]{2,1,0:T(8,128)(2,1)S(1)}, bf16[8,16,12000]{2,1,0:T(8,128)(2,1)}, u32[]{:S(2)}) %copy-start) | copy-done | bytes 3072024
  4.5 0.0 copy-start.1
  4.5 0.8 %copy-done.1 = f32[1,12000]{1,0:T(1,128)S(1)} copy-done((f32[1,12000]{1,0:T(1,128)S(1)}, f32[1,12000]{1,0:T(1,128)}, u32[]{:S(2)}) %copy-start.1) | copy-done | bytes 48024
  5.3 0.0 copy-start.2
  5.3 0.8 %copy-done.2 = bf16[128,128]{1,0:T(8,128)(2,1)S(1)} copy-done((bf16[128,128]{1,0:T(8,128)(2,1)S(1)}, bf16[128,128]{1,0:T(8,128)(2,1)}, u32[]{:S(2)}) %copy-start.2) | copy-done | bytes 32792
  6.0 12.0 %shard_map.91.own_ref = bf16[4,256,128]{2,1,0:T(8,128)(2,1)S(1)} custom-call(bf16[128,12000]{1,0:T(8,128)(2,1)S(1)} %bitcast.5, s32[128,1]{1,0:T(8,128)S(1)} %reshape.20.length_ref, f32[1,12000]{1,0:T(1,128)S(1)} %copy-done.1, bf16[128,128]{1,0:T(8,128)(2,1)S(1)} %copy-done.2, bf16[4,3072,256]{2,1,0:T(8,128)(2,1)} %constant.16.clone.table_ref), custom_call_target="tpu_custom_call" | custom-call | tf_op jit(solution)/shard_map/pallas_call | solution.py:348
  18.0 37.1 %shard_map.92 = bf16[8192,128]{1,0:T(8,128)(2,1)S(1)} custom-call(bf16[4,256,128]{2,1,0:T(8,128)(2,1)S(1)} %shard_map.91.own_ref, bf16[256,256]{1,0:T(8,128)(2,1)S(1)} %and_convert_fusion.place_ref), custom_call_target="tpu_custom_call" | custom-call | tf_op jit(solution)/shard_map/pallas_call | solution.py:379
  55.1 1.3 %copy.14 = bf16[512,8,2,128]{3,2,1,0:T(2,128)(2,1)} copy(bf16[512,8,2,128]{3,2,1,0:T(2,128)(2,1)S(1)} %bitcast.4) | data formatting | bytes 4194304
  (1 shorter events, 0.0 us)
Async XLA Ops:
  2.6 1.9 %copy-start = (bf16[8,16,12000]{2,1,0:T(8,128)(2,1)S(1)}, bf16[8,16,12000]{2,1,0:T(8,128)(2,1)}, u32[]{:S(2)}) copy-start(bf16[8,16,12000]{2,1,0:T(8,128)(2,1)} %param.9) | copy-start | bytes 9216004
  4.5 0.8 %copy-start.1 = (f32[1,12000]{1,0:T(1,128)S(1)}, f32[1,12000]{1,0:T(1,128)}, u32[]{:S(2)}) copy-start(f32[1,12000]{1,0:T(1,128)} %constant.14.clone.taper_ref) | copy-start | bytes 144004
  5.3 0.8 %copy-start.2 = (bf16[128,128]{1,0:T(8,128)(2,1)S(1)}, bf16[128,128]{1,0:T(8,128)(2,1)}, u32[]{:S(2)}) copy-start(bf16[128,128]{1,0:T(8,128)(2,1)} %constant.15.clone.order_ref) | copy-start | bytes 98308
